TPU v7x, 256 devices: a whole 4x4x8 slice. The times are simulated.
256 devices in a mesh: ctx: 64 (over y, z, x_lo), ch: 4 (over x_hi, core).
Axes of the slice: x: 4 (x_hi: 2, x_lo: 2; x = x_hi * 2 + x_lo), y: 4, z: 8, core: 2. Of those that a mesh axis runs over, the one named last changes fastest.
Arguments:
- base_ids: int32 [8192], P('ctx'), may hold values from 0 to 511
- base_table: bfloat16 [512, 3, 4096], P(None, None, 'ch'), may hold values from -6 to 6
- short_taps: float32 [3, 3, 4096], P(None, None, 'ch'), may hold values from -2.4 to 2.4
- mode_rates: float32 [16, 4096], P(None, 'ch'), may hold values from 3e-05 to 0.1
- mode_residues: float32 [16, 4096], P(None, 'ch'), may hold values from -1.8 to 1.8
- skip_gain: float32 [4096], P('ch'), may hold values from 0.5 to 1.5
- out_weight: bfloat16 [4096, 8192], P('ctx', 'ch'), may hold values from -0.09375 to 0.09375
Outputs:
- mixed: bfloat16 [8192, 8192], P('ctx', 'ch')
All inputs are finite; a program needn't handle non-finite values.
Results may differ from a plain program's by a relative error of at most 0.013.
Values may be sent and summed in bfloat16 or wider, within the bound.
A program may use at most 128 MiB of HBM per device.

v0:
```python
import jax
import jax.numpy as jnp
from jax import lax
from jax.sharding import PartitionSpec as P

block_len = 32


def shifted(value, axis, steps):
    count = lax.axis_size(axis)
    leading, last = (max(0, -steps), min(count, count - steps))
    return lax.ppermute(value, axis, [(source, source + steps) for source in range(leading, last)])


def chain(earlier, later):
    return (earlier[0] * later[0], earlier[1] * later[0] + later[1])


def mode_tables(rates, residues):
    coef = residues * jnp.sqrt(2.0 * rates)
    lags = jnp.arange(block_len).astype(jnp.float32)
    decay = jnp.exp(-rates[:, :, None] * lags[None, None, :])
    filt = jnp.sum(coef[:, :, None] * decay, axis=0)
    offset = jnp.arange(block_len)[:, None] - jnp.arange(block_len)[None, :]
    toeplitz = jnp.where(offset[None, :, :] >= 0, filt[:, jnp.clip(offset, 0, block_len - 1)], 0.0)
    end_weight = jnp.exp(-rates[:, :, None] * (block_len - 1 - lags)[None, None, :])
    out_weight_modes = coef[:, :, None] * jnp.exp(-rates[:, :, None] * (lags + 1.0)[None, None, :])
    return (toeplitz, end_weight, out_weight_modes)


def block_pass(signal, rates, tables):
    toeplitz, end_weight, out_modes = tables
    width, length = signal.shape
    blocks = length // block_len
    shaped = signal.reshape(width, blocks, block_len)
    inner = jnp.einsum("cts,cbs->cbt", toeplitz, shaped, precision=lax.Precision.HIGHEST)
    ends = jnp.einsum("rcs,cbs->rcb", end_weight, shaped, precision=lax.Precision.HIGHEST)
    steps = jnp.broadcast_to(jnp.exp(-rates * block_len)[:, :, None], ends.shape)
    scanned = lax.associative_scan(chain, (steps, ends), axis=2)[1]
    before = jnp.concatenate([jnp.zeros_like(scanned[:, :, :1]), scanned[:, :, :-1]], axis=2)
    index_f = jnp.arange(blocks).astype(jnp.float32)
    decay_before = jnp.exp(-rates[:, :, None] * (block_len * index_f)[None, None, :])
    return (inner, before, decay_before, scanned[:, :, -1])


def finish(parts, start, out_modes):
    inner, before, decay_before, last = parts
    width, blocks = (inner.shape[0], inner.shape[1])
    states = before + decay_before * start[:, :, None]
    outer = jnp.einsum("rct,rcb->cbt", out_modes, states, precision=lax.Precision.HIGHEST)
    return (inner + outer).reshape(width, blocks * block_len)


def body(base_ids, base_table, short_taps, mode_rates, mode_residues, skip_gain, out_weight):
    rows = jnp.take(base_table, base_ids, axis=0)
    prior = shifted(rows[-2:], "ctx", 1)
    padded = jnp.concatenate([prior, rows], axis=0).astype(jnp.float32)
    feat = short_taps[0] * padded[2:] + short_taps[1] * padded[1:-1] + short_taps[2] * padded[:-2]
    query = feat[:, 0]
    product = (feat[:, 1] * feat[:, 2]).astype(jnp.bfloat16)
    product_f = product.astype(jnp.float32)
    local_ch = product.shape[1]
    sub_width = local_ch // lax.axis_size("ctx")
    first = lax.axis_index("ctx") * sub_width
    rates_sub = lax.dynamic_slice_in_dim(mode_rates, first, sub_width, 1)
    residues_sub = lax.dynamic_slice_in_dim(mode_residues, first, sub_width, 1)
    whole = lax.all_to_all(product.T, "ctx", split_axis=0, concat_axis=1, tiled=True).astype(
        jnp.float32
    )
    tables = mode_tables(rates_sub, residues_sub)
    parts = block_pass(whole, rates_sub, tables)
    convolved_ch = finish(parts, jnp.zeros_like(rates_sub), tables[2])
    convolved = lax.all_to_all(convolved_ch, "ctx", split_axis=1, concat_axis=0, tiled=True).T
    gated = (query * (convolved + skip_gain * product_f)).astype(jnp.bfloat16)
    gathered = lax.all_gather(gated, "ch", axis=1, tiled=True)
    total = jnp.dot(
        gathered,
        lax.all_gather(out_weight, "ctx", axis=0, tiled=True),
        preferred_element_type=jnp.float32,
    )
    return total.astype(jnp.bfloat16)


def solution(mesh):
    in_specs = (
        P("ctx"),
        P(None, None, "ch"),
        P(None, None, "ch"),
        P(None, "ch"),
        P(None, "ch"),
        P("ch"),
        P("ctx", "ch"),
    )
    out_specs = P("ctx", "ch")
    return jax.shard_map(body, mesh=mesh, in_specs=in_specs, out_specs=out_specs, check_vma=False)
```

profile of v0, /device:TPU:8, one launch (start us, length us, event | category | flops | bytes accessed | tf_op | source)
XLA Modules:
  0.0 696.0 jit_solution(5693877176848301776)
XLA Ops:
  8.4 3.9 gather_fusion
  14.5 3.4 collective-permute-start
  28.6 12.5 %all-to-all-start = ((bf16[64,16,128]{2,1,0:T(8,128)(2,1)}), bf16[64,16,128]{2,1,0:T(8,128)(2,1)S(1)}, u32[]{:S(2)}, u32[]{:S(2)}) async-start(bf16[64,16,128]{2,1,0:T(8,128)(2,1)} %bitcast.55), calls=%async_computation | async-start | bytes 524288 | tf_op jit(solution)/shard_map/all_to_all | solution.py:67
  41.6 4.0 gather_fusion.1
  45.7 2.0 copy.91
  49.4 3.0 all-to-all-done
  55.5 2.2 convolution_bitcast_fusion
  57.7 4.5 slice.211
  62.2 5.1 slice.213
  68.3 2.3 slice.215
  70.7 3.0 slice.217
  74.6 1.8 slice.219
  76.5 1.9 slice.221
  82.0 1.7 multiply_add_fusion.3
  83.7 1.8 slice.227
  85.6 1.9 slice.229
  87.5 1.7 multiply_add_fusion.2
  89.2 1.7 slice.231
  90.9 1.7 slice.233
  97.1 1.8 slice.249
  99.0 2.1 slice.252
  101.1 1.8 slice.255
  102.9 2.9 slice.258
  105.8 5.9 slice.261
  115.4 6.2 pad.53
  121.6 1.7 pad_maximum_fusion
  123.4 8.8 %pad.52 = f32[16,16,4]{2,0,1:T(8,128)} pad(f32[16,16,2]{2,0,1:T(8,128)} %pad_maximum_fusion, f32[]{:T(128)} %constant.9.clone.1), padding=0_0_0x0_0_0x0_1_1 | pad | bytes 6148 | tf_op jit(solution)/shard_map/pad | solution.py:39
  135.8 6.1 pad.54
  141.9 8.8 %pad.55 = f32[16,16,8]{2,0,1:T(8,128)} pad(f32[16,16,4]{2,0,1:T(8,128)} %add.170, f32[]{:T(128)} %constant.9.clone.1), padding=0_0_0x0_0_0x1_0_1 | pad | bytes 12292 | tf_op jit(solution)/shard_map/pad | solution.py:39
  152.3 8.9 %pad.57 = f32[16,16,16]{2,0,1:T(8,128)} pad(f32[16,16,8]{2,0,1:T(8,128)} %add.172, f32[]{:T(128)} %constant.9.clone.1), padding=0_0_0x0_0_0x1_0_1 | pad | bytes 24580 | tf_op jit(solution)/shard_map/pad | solution.py:39
  164.0 8.9 %pad.56 = f32[16,16,16]{2,0,1:T(8,128)} pad(f32[16,16,8]{2,0,1:T(8,128)} %pad_maximum_fusion.2, f32[]{:T(128)} %constant.9.clone.1), padding=0_0_0x0_0_0x0_1_1 | pad | bytes 24580 | tf_op jit(solution)/shard_map/pad | solution.py:39
  176.4 6.5 pad.58
  182.9 9.0 %pad.59 = f32[16,16,32]{2,0,1:T(8,128)} pad(f32[16,16,16]{2,0,1:T(8,128)} %add.174, f32[]{:T(128)} %constant.9.clone.1), padding=0_0_0x0_0_0x1_0_1 | pad | bytes 49156 | tf_op jit(solution)/shard_map/pad | solution.py:39
  193.4 9.2 %pad.61 = f32[16,16,64]{2,0,1:T(8,128)} pad(f32[16,16,32]{2,0,1:T(8,128)} %add.176, f32[]{:T(128)} %constant.9.clone.1), padding=0_0_0x0_0_0x1_0_1 | pad | bytes 98308 | tf_op jit(solution)/shard_map/pad | solution.py:39
  203.8 2.1 pad.60
  208.7 3.2 pad.62
  211.9 7.4 %pad.63 = f32[16,16,128]{2,0,1:T(8,128)S(1)} pad(f32[16,16,64]{2,0,1:T(8,128)} %add.178, f32[]{:T(128)} %constant.9.clone.1), padding=0_0_0x0_0_0x1_0_1 | pad | bytes 196612 | tf_op jit(solution)/shard_map/pad | solution.py:39
  220.0 10.5 %pad.108 = f32[16,16,256]{2,0,1:T(8,128)} pad(f32[16,16,128]{2,0,1:T(8,128)} %add.180, f32[]{:T(128)} %constant.9.clone.1), padding=0_0_0x0_0_0x1_0_1 | pad | bytes 393220
  232.3 10.5 %pad.85 = f32[16,16,255]{2,0,1:T(8,128)} pad(f32[16,16,128]{2,0,1:T(8,128)} %pad_maximum_fusion.6, f32[]{:T(128)} %constant.9.clone.1), padding=0_0_0x0_0_0x0_0_1 | pad | bytes 392196 | tf_op jit(solution)/shard_map/slice | solution.py:40
  245.5 1.9 convolution_add_fusion
  247.5 3.0 copy.110
  250.5 2.7 all_to_all.29
  254.5 24.2 %all_to_all.35 = f32[16,64,128]{2,0,1:T(8,128)} all-to-all(f32[16,64,128]{2,0,1:T(8,128)S(1)} %copy.111), channel_id=1, replica_groups=mesh['ctx'=64,'ch'=4] {'ctx'}, dimensions={1} | all-to-all | bytes 1048576 | tf_op jit(solution)/shard_map/all_to_all | solution.py:73
  278.7 2.0 copy.112
  280.8 2.4 fusion.4
  283.9 19.8 %all-gather.3.cloned.1.call-done = bf16[128,4096]{1,0:T(8,128)(2,1)} async-done(((bf16[128,1024]{1,0:T(8,128)(2,1)}), bf16[128,4096]{1,0:T(8,128)(2,1)}) %all-gather.3.cloned.1.call-update) | async-done | bytes 1048592 | tf_op jit(solution)/shard_map/all_gather | solution.py:75
  303.7 376.2 %all-gather.5.cloned.1.call-done = bf16[4096,2048]{1,0:T(8,128)(2,1)} async-done(((bf16[64,2048]{1,0:T(8,128)(2,1)}), bf16[4096,2048]{1,0:T(8,128)(2,1)}) %all-gather.5.cloned.1.call-update) | async-done | bytes 16777232 | tf_op jit(solution)/shard_map/all_gather | solution.py:78
  679.9 9.2 %convolution_convert_fusion = bf16[128,2048]{1,0:T(8,128)(2,1)} fusion(bf16[128,4096]{1,0:T(8,128)(2,1)} %all-gather.3.cloned.1.call-done, bf16[4096,2048]{1,0:T(8,128)(2,1)} %all-gather.5.cloned.1.call-done), kind=kOutput, calls=%fused_computation.2 | convolution fusion | flops 2147745792 | bytes 18350080 | tf_op jit(solution)/shard_map/dot_general | solution.py:76
  (106 shorter events, 58.3 us)
Async XLA Ops:
  6.5 1.9 copy-start
  12.3 5.6 copy-start.12
  13.6 0.9 copy-start.5
  14.5 10.2 %collective-permute-start = (bf16[2,3,1024]{2,0,1:T(2,128)(2,1)S(1)}, bf16[2,3,1024]{2,0,1:T(2,128)(2,1)S(1)}, u32[]{:S(2)}, u32[]{:S(2)}) collective-permute-start(bf16[2,3,1024]{2,0,1:T(2,128)(2,1)S(1)} %slice.267), channel_id=1, source_target_pairs={{0,4},{4,8},{8,12},{12,16},{16,20},{20,24},{24,28},{28,32},{32,36}... | collective-permute-start | bytes 36872 | tf_op jit(solution)/shard_map/ppermute | solution.py:12
  24.7 16.7 %copy-start.10 = (f32[16,16]{0,1:T(8,128)}, f32[16,16]{0,1:T(8,128)S(1)}, u32[]{:S(2)}) copy-start(f32[16,16]{0,1:T(8,128)S(1)} %copy.88) | copy-start | bytes 3076
  26.6 1.1 copy-start.1
  28.6 23.7 %all-to-all-start = ((bf16[64,16,128]{2,1,0:T(8,128)(2,1)}), bf16[64,16,128]{2,1,0:T(8,128)(2,1)S(1)}, u32[]{:S(2)}, u32[]{:S(2)}) async-start(bf16[64,16,128]{2,1,0:T(8,128)(2,1)} %bitcast.55), calls=%async_computation | async-start | bytes 524288 | tf_op jit(solution)/shard_map/all_to_all | solution.py:67
  41.2 262.6 %all-gather.3.cloned.1.call-start = ((), (), s32[]{:S(2)}) async-start(), calls=%async_computation.2 | async-start | bytes 1310720 | tf_op jit(solution)/shard_map/all_gather | solution.py:75
  52.4 0.7 copy-start.8
  57.7 4.5 copy-start.6
  79.4 11.5 %copy-start.3 = (f32[16,16,32]{2,0,1:T(8,128)}, f32[16,16,32]{2,0,1:T(8,128)S(1)}, u32[]{:S(2)}) copy-start(f32[16,16,32]{2,0,1:T(8,128)S(1)} %multiply_add_fusion.4) | copy-start | bytes 98308
  111.7 2.9 copy-start.9
  141.9 33.8 %copy-start.4 = (f32[16,16,32]{2,0,1:T(8,128)S(1)}, f32[16,16,32]{2,0,1:T(8,128)}, u32[]{:S(2)}) copy-start(f32[16,16,32]{2,0,1:T(8,128)} %copy-done.3) | copy-start | bytes 98308
  205.9 25.6 %slice-start = ((f32[16,16,256]{2,0,1:T(8,128)}), f32[16,16,1]{2,0,1:T(8,128)S(1)}, s32[]{:S(2)}) async-start(f32[16,16,256]{2,0,1:T(8,128)} %copy-done.6), calls=%async_computation.4 | async-start | bytes 262144 | tf_op jit(solution)/shard_map/slice | solution.py:39
  231.5 12.5 %copy-start.11 = (f32[16,16]{0,1:T(8,128)S(1)}, f32[16,16]{0,1:T(8,128)}, u32[]{:S(2)}) copy-start(f32[16,16]{0,1:T(8,128)} %copy-done.10) | copy-start | bytes 3076
  231.5 14.0 %copy-start.7 = (f32[32,32,16]{1,0,2:T(8,128)S(1)}, f32[32,32,16]{1,0,2:T(8,128)}, u32[]{:S(2)}) copy-start(f32[32,32,16]{1,0,2:T(8,128)} %copy.91) | copy-start | bytes 196612
  232.3 13.2 %copy-start.13 = (pred[32,32]{1,0:T(8,128)(4,1)S(1)}, pred[32,32]{1,0:T(8,128)(4,1)}, u32[]{:S(2)}) copy-start(pred[32,32]{1,0:T(8,128)(4,1)} %subtract_compare_fusion) | copy-start | bytes 3076
  242.8 2.8 copy-start.2
  253.1 27.6 %copy-start.14 = (f32[1024]{0:T(1024)S(1)}, f32[1024]{0:T(1024)}, u32[]{:S(2)}) copy-start(f32[1024]{0:T(1024)} %param.12) | copy-start | bytes 12292
  283.2 396.8 %all-gather.5.cloned.1.call-start = ((), (), s32[]{:S(2)}) async-start(), calls=%async_computation.3 | async-start | bytes 17039360 | tf_op jit(solution)/shard_map/all_gather | solution.py:78
Sparse Core Ops, SparseCore 0:
  283.3 20.3 all-gather.2
  305.5 374.3 all-gather.4
where the time goes:
time: 703 us; the launch traced here: 696 us
  waiting for transfers between devices  400 us (57%)
  local copies, waits for them, and re-layouts  184 us (26%)
  other arithmetic  43.5 us (6%)
  blocking collectives  24.2 us (3%)
  starting transfers between devices  16.2 us (2%)
  matrix products  14.9 us (2%)
  between operations  13.8 us (2%)
    all_gather x1, waiting for transfers between devices, body(): lax.all_gather(out_weight, 'ctx', axis=0, tiled=True)  376 us
    pad x12, local copies, waits for them, and re-layouts, block_pass(): scanned = lax.associative_scan(chain, (steps, ends), axis=2)[1]  85 us
    slice x24, local copies, waits for them, and re-layouts, block_pass(): scanned = lax.associative_scan(chain, (steps, ends), axis=2)[1]  48 us
    all_to_all x1, blocking collectives, body(): lax.all_to_all(convolved_ch, 'ctx', split_axis=1, concat_axis=0, tiled=True)  24.2 us
    all_gather x1, waiting for transfers between devices, body(): gathered = lax.all_gather(gated, 'ch', axis=1, tiled=True)  19.8 us
    add x14, other arithmetic, chain(): return (earlier[0] * later[0], earlier[1] * later[0] + later[1])  16.1 us
  transfers between devices with their start and end apart: 4, of which 3 were waited for; matrix products, arithmetic and copies ran while one was open for 2% of the time, Pallas kernels for 0%

commit v1 on v0

v1 whole, which is shorter than its diff:
```python
import functools
import jax
import jax.numpy as jnp
from jax import lax
from jax.experimental import pallas as pl
from jax.experimental.pallas import tpu as pltpu
from jax.sharding import PartitionSpec as P

MESH = pl.DeviceIdType.MESH
NY, NZ, NX, NCH = 4, 8, 2, 4
PLANE = NZ * NX
T = 128
CL = 1024
LT = CL // 128
R = 16
KS = 64
NL = 2048
NCHUNK = 8
CW = NL // NCHUNK
HW = CW // 2
PAIRED = (0, 1, 2, 3)
SHARD = (4, 5, 6, 7)
ORDER = (0, 4, 1, 5, 2, 6, 3, 7)


def right_steps(n):
    return 4 if n % 2 == 0 else 3


def left_steps(n):
    return NZ - 1 - right_steps(n)


def kernel(
    ids_ref, taps_ref, rates_ref, res_ref, skip_ref, table_hbm, w_hbm, out_ref,
    table, rows, halo_out, halo_in, q_ref, u_ref, u2d, z2d, rate_t, coef_t,
    e_out, e_in, s_out, s_in, tot_out, tot_in, ybf, ybuf, wbuf,
    o_stage, relay_in, f32_part, fin_out, fin_in,
    sem_table, sem_w, halo_s, halo_r, e_s, e_r, t_s, t_r, b_s, b_r,
    yx_s, yx_r, yc_s, yc_r, yl_s, wx_s, wx_r, wz_s, wz_r,
    rl_s, rl_r, fn_s, fn_r,
):
    f32 = jnp.float32
    i = lax.axis_index("ctx")
    c = lax.axis_index("ch")
    y = i // PLANE
    p = lax.rem(i, PLANE)
    z = p // NX
    xl = lax.rem(p, NX)

    def in_plane(q):
        return (y * PLANE + q, c)

    def at(yy, cc):
        return (yy * PLANE + p, cc)

    def rdma(src, dst, ss, rs, dev):
        return pltpu.make_async_remote_copy(
            src_ref=src, dst_ref=dst, send_sem=ss, recv_sem=rs, device_id=dev, device_id_type=MESH
        )

    bar = pltpu.get_barrier_semaphore()
    n_peers = 0
    for d in range(1, PLANE):
        pl.semaphore_signal(bar, inc=1, device_id=in_plane(lax.rem(p + d, PLANE)), device_id_type=MESH)
        n_peers += 1
    for dy in range(NY):
        for dc in range(NCH):
            if dy or dc:
                pl.semaphore_signal(
                    bar, inc=1, device_id=at(lax.rem(y + dy, NY), lax.rem(c + dc, NCH)), device_id_type=MESH
                )
                n_peers += 1
    nxt, prv = lax.rem(i + 1, NY * PLANE), lax.rem(i + NY * PLANE - 1, NY * PLANE)
    for other in (nxt, prv):
        pl.semaphore_signal(bar, inc=1, device_id=(other, c), device_id_type=MESH)
        n_peers += 1

    def table_copy(w):
        return pltpu.make_async_copy(table_hbm.at[w], table.at[w], sem_table.at[w])

    own_row = pl.multiple_of(p * KS, KS)

    def w_copy(n):
        return pltpu.make_async_copy(
            w_hbm.at[:, pl.ds(n * CW, CW)], wbuf.at[n, pl.ds(own_row, KS), :], sem_w.at[n]
        )

    for w in (1, 2, 0):
        table_copy(w).start()
    for n in ORDER:
        w_copy(n).start()

    for lt in range(LT):
        cols = slice(lt * 128, (lt + 1) * 128)
        rt = rates_ref[:, cols]
        rate_t[pl.ds(lt, R, stride=LT), :] = rt
        coef_t[pl.ds(lt, R, stride=LT), :] = res_ref[:, cols] * jnp.sqrt(2.0 * rt)

    ids_f = jnp.broadcast_to(ids_ref[...].astype(f32), (T, T))
    ids_col = jnp.transpose(ids_f)
    lane = lax.broadcasted_iota(jnp.int32, (T, T), 1).astype(f32)
    onehot = jnp.concatenate(
        [jnp.where(ids_col == lane + float(128 * j), 1.0, 0.0).astype(jnp.bfloat16) for j in range(4)], axis=1
    )
    for w in (1, 2, 0):
        table_copy(w).wait()
        for h in range(4):
            cols = slice(h * 256, (h + 1) * 256)
            rows[w, 8:, cols] = jnp.dot(onehot, table[w, :, cols], preferred_element_type=f32)
        halo_out[w, :, :] = rows[w, 8 + T - 2:, :]

    pl.semaphore_wait(bar, n_peers)

    halo = rdma(halo_out, halo_in, halo_s, halo_r, (nxt, c))
    halo.start()

    partner = in_plane(p + 1 - 2 * xl)
    zr = in_plane(lax.rem(z + 1, NZ) * NX + xl)
    zl = in_plane(lax.rem(z + NZ - 1, NZ) * NX + xl)

    def w_rows(n, zz):
        if n in PAIRED:
            return wbuf.at[n, pl.ds(pl.multiple_of(zz * (2 * KS), 2 * KS), 2 * KS), :]
        return wbuf.at[n, pl.ds(pl.multiple_of(zz * (2 * KS) + xl * KS, KS), KS), :]

    def zat(d):
        return lax.rem(z + d + NZ, NZ)

    def w_x(n, zz):
        ref = wbuf.at[n, pl.ds(pl.multiple_of(zz * (2 * KS) + xl * KS, KS), KS), :]
        return ref

    def x_copy(n, d):
        ref = w_x(n, zat(d))
        return rdma(ref, ref, wx_s.at[n, d % NZ], wx_r.at[n, d % NZ], partner)

    def ring(n, direction, s):
        ref = w_rows(n, zat(-s if direction == 0 else s))
        return rdma(ref, ref, wz_s.at[n, direction, s], wz_r.at[n, direction, s], zr if direction == 0 else zl)

    for n in ORDER:
        w_copy(n).wait()
        if n in PAIRED:
            x_copy(n, 0).start()

    def w_op(n, s):
        steps = (right_steps(n), left_steps(n))
        if s == 0:
            if n in PAIRED:
                x_copy(n, 0).wait_recv()
            for direction in (0, 1):
                ring(n, direction, 0).start()
            if n not in PAIRED:
                x_copy(n, 0).start()
            return
        for direction in (0, 1):
            if s - 1 < steps[direction]:
                ring(n, direction, s - 1).wait_recv()
                if s < steps[direction]:
                    ring(n, direction, s).start()
                if n not in PAIRED:
                    x_copy(n, -s if direction == 0 else s).start()

    def w_done(n):
        if n not in PAIRED:
            for d in range(NZ):
                x_copy(n, d).wait_recv()

    ops = sorted(
        [(2 * (n % 4) + s, n % 4, n, s) for n in ORDER for s in range(5)]
    )
    ops = [(n, s) for _, _, n, s in ops]
    state = {"next": 0}

    def advance(upto):
        while state["next"] < len(ops) and upto(state["next"], ops[state["next"]]):
            w_op(*ops[state["next"]])
            state["next"] += 1

    def advance_to(k):
        advance(lambda idx, op: idx < k)

    def features(t0, n):
        for lt in range(LT):
            cols = slice(lt * 128, (lt + 1) * 128)
            feat = []
            for w in range(3):
                acc = taps_ref[0, w:w + 1, cols] * rows[w, 8 + t0:8 + t0 + n, cols]
                acc += taps_ref[1, w:w + 1, cols] * rows[w, 7 + t0:7 + t0 + n, cols]
                acc += taps_ref[2, w:w + 1, cols] * rows[w, 6 + t0:6 + t0 + n, cols]
                feat.append(acc)
            q_ref[t0:t0 + n, cols] = feat[0]
            u = (feat[1] * feat[2]).astype(jnp.bfloat16).astype(f32)
            u_ref[t0:t0 + n, cols] = u
            u2d[pl.ds(t0 * LT + lt, n, stride=LT), :] = u

    features(8, T - 8)

    rate = [rate_t[r * LT:(r + 1) * LT, :] for r in range(R)]
    decay = [jnp.exp(-v) for v in rate]

    def scan_states(lo, hi, init):
        def step(b, carry):
            s = list(carry)
            for k in range(8):
                u = u2d[pl.ds(pl.multiple_of((b * 8 + k) * LT, LT), LT), :]
                s = [s[r] * decay[r] + u for r in range(R)]
            return tuple(s)

        return lax.fori_loop(lo, hi, step, init)

    zero = jnp.zeros((LT, 128), f32)
    tail = scan_states(1, T // 8, (zero,) * R)
    for r in range(R):
        e_out[r] = tail[r]

    halo.wait_recv()
    keep = jnp.where(i == 0, 0.0, 1.0).astype(f32)
    for w in range(3):
        rows[w, 6:8, :] = halo_in[w, :, :] * keep
    features(0, 8)
    head = scan_states(0, 1, (zero,) * R)
    for r in range(R):
        e_out[r] = e_out[r] + jnp.exp(-float(T - 8) * rate[r]) * head[r]

    def e_copy(d):
        to = lax.rem(p + d, PLANE)
        return rdma(e_out.at[to], e_in.at[p], e_s.at[d], e_r.at[p], in_plane(to))

    def e_from(d):
        frm = lax.rem(p + d, PLANE)
        return rdma(e_out.at[frm], e_in.at[frm], e_s.at[d], e_r.at[frm], in_plane(frm))

    for d in range(1, PLANE):
        e_copy(d).start()
    e_in[p] = e_out[p]
    advance_to(4)
    for d in range(1, PLANE):
        e_from(d).wait_recv()

    my_rate = rate_t[pl.ds(pl.multiple_of(p * LT, LT), LT), :]
    dev_decay = jnp.exp(-float(T) * my_rate)
    pref = zero
    prefs = []
    for j in range(PLANE):
        prefs.append(pref)
        pref = pref * dev_decay + e_in[j]
    tot_out[...] = pref

    def t_copy(d):
        to = lax.rem(y + d, NY)
        return rdma(tot_out, tot_in.at[y], t_s.at[d], t_r.at[y], at(to, c))

    def t_from(d):
        frm = lax.rem(y + d, NY)
        return rdma(tot_out, tot_in.at[frm], t_s.at[d], t_r.at[frm], at(frm, c))

    for d in range(1, NY):
        t_copy(d).start()
    tot_in[y] = pref
    advance_to(8)
    for d in range(1, NY):
        t_from(d).wait_recv()
    carry = zero
    for yy in range(NY - 1):
        gap = jnp.maximum(y - 1 - yy, 0).astype(f32) * float(PLANE * T)
        carry = carry + jnp.where(yy < y, jnp.exp(-gap * my_rate) * tot_in[yy], 0.0)
    for j in range(PLANE):
        s_out[j] = prefs[j] + jnp.exp(-float(T * j) * my_rate) * carry

    def s_copy(d):
        to = lax.rem(p + d, PLANE)
        return rdma(s_out.at[to], s_in.at[p], b_s.at[d], b_r.at[p], in_plane(to))

    def s_from(d):
        frm = lax.rem(p + d, PLANE)
        return rdma(s_out.at[frm], s_in.at[frm], b_s.at[d], b_r.at[frm], in_plane(frm))

    for d in range(1, PLANE):
        s_copy(d).start()
    s_in[p] = s_out[p]
    advance_to(12)
    for d in range(1, PLANE):
        s_from(d).wait_recv()

    coef = [coef_t[r * LT:(r + 1) * LT, :] for r in range(R)]

    def out_step(b, carry):
        s = list(carry)
        for k in range(4):
            at_t = pl.ds(pl.multiple_of((b * 4 + k) * LT, LT), LT)
            u = u2d[at_t, :]
            s = [s[r] * decay[r] + u for r in range(R)]
            terms = [s[r] * coef[r] for r in range(R)]
            while len(terms) > 1:
                terms = [terms[m] + terms[m + 1] for m in range(0, len(terms), 2)]
            z2d[at_t, :] = terms[0]
        return tuple(s)

    lax.fori_loop(0, T // 4, out_step, tuple(s_in[r] for r in range(R)))

    for lt in range(LT):
        cols = slice(lt * 128, (lt + 1) * 128)
        conv = z2d[pl.ds(lt, T, stride=LT), :]
        gated = q_ref[:, cols] * (conv + skip_ref[:, cols] * u_ref[:, cols])
        ybf[:, cols] = gated.astype(jnp.bfloat16)

    odd = lax.rem(y, 2)
    core = lax.rem(c, 2)

    def y_copy(h):
        return rdma(ybf, ybuf.at[y], yx_s.at[h], yx_r.at[y], at(c, 2 * h + odd))

    def y_own():
        return pltpu.make_async_copy(ybf, ybuf.at[y], yl_s)

    def is_self(h):
        return jnp.logical_and(y == c, c // 2 == h)

    for h in range(2):
        @pl.when(jnp.logical_not(is_self(h)))
        def _():
            y_copy(h).start()

    mine = y == c

    @pl.when(mine)
    def _():
        y_own().start()
        y_own().wait()

    advance_to(16)
    sib = at(y, c + 1 - 2 * core)

    def y_cross(k):
        slot = 2 * k + core
        return rdma(ybuf.at[slot], ybuf.at[slot], yc_s.at[k], yc_r.at[slot], sib)

    def y_cross_from(k):
        slot = 2 * k + 1 - core
        return rdma(ybuf.at[slot], ybuf.at[slot], yc_s.at[k], yc_r.at[slot], sib)

    for k in range(2):
        slot = 2 * k + core

        @pl.when(jnp.logical_not(jnp.logical_and(slot == y, c == y)))
        def _():
            rdma(ybf, ybuf.at[slot], yx_s.at[k], yx_r.at[slot], at(slot, y)).wait_recv()

        y_cross(k).start()
    for k in range(2):
        y_cross_from(k).wait_recv()

    yr, yl = at(lax.rem(y + 1, NY), c), at(lax.rem(y + NY - 1, NY), c)
    A, B = slice(0, HW), slice(HW, CW)

    def relay(n, side):
        return rdma(o_stage.at[n, side], relay_in.at[n, side], rl_s.at[n, side], rl_r.at[n, side], (yr, yl)[side])

    def final(n, side):
        return rdma(fin_out.at[n, side], fin_in.at[n, side], fn_s.at[n, side], fn_r.at[n, side], (yr, yl)[side])

    def product(n, d):
        block = ybuf[lax.rem(y + d, NY)]
        return jnp.dot(block, wbuf[n], preferred_element_type=f32)

    def stage1(n):
        advance(lambda idx, op: any(m == n for m, _ in ops[idx:]))
        w_done(n)
        far = product(n, 2)
        o_stage[n, 0] = far[:, A].astype(jnp.bfloat16)
        o_stage[n, 1] = far[:, B].astype(jnp.bfloat16)
        relay(n, 0).start()
        relay(n, 1).start()
        f32_part[n, 0] = product(n, 1)
        f32_part[n, 1] = product(n, 3)
        f32_part[n, 2] = product(n, 0)

    def stage2(n):
        relay(n, 0).wait_recv()
        fin_out[n, 0, :, A] = (f32_part[n, 0, :, A] + relay_in[n, 0].astype(f32)).astype(jnp.bfloat16)
        fin_out[n, 0, :, B] = f32_part[n, 0, :, B].astype(jnp.bfloat16)
        final(n, 0).start()
        relay(n, 1).wait_recv()
        fin_out[n, 1, :, A] = f32_part[n, 1, :, A].astype(jnp.bfloat16)
        fin_out[n, 1, :, B] = (f32_part[n, 1, :, B] + relay_in[n, 1].astype(f32)).astype(jnp.bfloat16)
        final(n, 1).start()

    def stage3(n):
        final(n, 0).wait_recv()
        final(n, 1).wait_recv()
        total = f32_part[n, 2] + fin_in[n, 0].astype(f32) + fin_in[n, 1].astype(f32)
        out_ref[:, n * CW:(n + 1) * CW] = total.astype(jnp.bfloat16)

    for k, n in enumerate(ORDER):
        stage1(n)
        if k >= 1:
            stage2(ORDER[k - 1])
        if k >= 3:
            stage3(ORDER[k - 3])
    stage2(ORDER[-1])
    for n in ORDER[-3:]:
        stage3(n)

    halo.wait_send()
    for d in range(1, PLANE):
        e_copy(d).wait_send()
        s_copy(d).wait_send()
    for d in range(1, NY):
        t_copy(d).wait_send()
    for h in range(2):
        @pl.when(jnp.logical_not(is_self(h)))
        def _():
            y_copy(h).wait_send()
    for k in range(2):
        y_cross(k).wait_send()
    for n in ORDER:
        for direction, steps in ((0, right_steps(n)), (1, left_steps(n))):
            for s in range(steps):
                ring(n, direction, s).wait_send()
        if n in PAIRED:
            x_copy(n, 0).wait_send()
        else:
            for d in range(NZ):
                x_copy(n, d).wait_send()
        for side in range(2):
            relay(n, side).wait_send()
            final(n, side).wait_send()


def body(base_ids, base_table, short_taps, mode_rates, mode_residues, skip_gain, out_weight):
    f32, bf = jnp.float32, jnp.bfloat16
    table = jnp.transpose(base_table, (1, 0, 2))
    vmem = pl.BlockSpec(memory_space=pltpu.VMEM)
    hbm = pl.BlockSpec(memory_space=pl.ANY)
    dma = pltpu.SemaphoreType.DMA
    scratch = [
        pltpu.VMEM((3, 512, CL), bf),
        pltpu.VMEM((3, T + 8, CL), f32),
        pltpu.VMEM((3, 2, CL), f32),
        pltpu.VMEM((3, 2, CL), f32),
        pltpu.VMEM((T, CL), f32),
        pltpu.VMEM((T, CL), f32),
        pltpu.VMEM((T * LT, 128), f32),
        pltpu.VMEM((T * LT, 128), f32),
        pltpu.VMEM((R * LT, 128), f32),
        pltpu.VMEM((R * LT, 128), f32),
        pltpu.VMEM((R, LT, 128), f32),
        pltpu.VMEM((R, LT, 128), f32),
        pltpu.VMEM((R, LT, 128), f32),
        pltpu.VMEM((R, LT, 128), f32),
        pltpu.VMEM((LT, 128), f32),
        pltpu.VMEM((NY, LT, 128), f32),
        pltpu.VMEM((T, CL), bf),
        pltpu.VMEM((NY, T, CL), bf),
        pltpu.VMEM((NCHUNK, CL, CW), bf),
        pltpu.VMEM((NCHUNK, 2, T, HW), bf),
        pltpu.VMEM((NCHUNK, 2, T, HW), bf),
        pltpu.VMEM((NCHUNK, 3, T, CW), f32),
        pltpu.VMEM((NCHUNK, 2, T, CW), bf),
        pltpu.VMEM((NCHUNK, 2, T, CW), bf),
        dma((3,)), dma((NCHUNK,)),
        dma, dma,
        dma((PLANE,)), dma((PLANE,)),
        dma((NY,)), dma((NY,)),
        dma((PLANE,)), dma((PLANE,)),
        dma((2,)), dma((NY,)), dma((2,)), dma((NY,)), dma,
        dma((NCHUNK, NZ)), dma((NCHUNK, NZ)),
        dma((NCHUNK, 2, 4)), dma((NCHUNK, 2, 4)),
        dma((NCHUNK, 2)), dma((NCHUNK, 2)),
        dma((NCHUNK, 2)), dma((NCHUNK, 2)),
    ]
    return pl.pallas_call(
        kernel,
        out_shape=jax.ShapeDtypeStruct((T, NL), bf),
        in_specs=[vmem] * 5 + [hbm] * 2,
        out_specs=vmem,
        scratch_shapes=scratch,
        compiler_params=pltpu.CompilerParams(
            collective_id=0, has_side_effects=True, vmem_limit_bytes=56 * 2**20
        ),
        name="mixer",
    )(
        base_ids.reshape(1, T), short_taps, mode_rates, mode_residues,
        skip_gain.reshape(1, CL), table, out_weight,
    )


def solution(mesh):
    in_specs = (
        P("ctx"),
        P(None, None, "ch"),
        P(None, None, "ch"),
        P(None, "ch"),
        P(None, "ch"),
        P("ch"),
        P("ctx", "ch"),
    )
    return jax.shard_map(body, mesh=mesh, in_specs=in_specs, out_specs=P("ctx", "ch"), check_vma=False)
```

time: 703 us -> 94.5 us (0.13)
  waiting for transfers between devices: 400 us -> 0 us
  local copies, waits for them, and re-layouts: 184 us -> 1.88 us
  Pallas kernels: 0 us -> 92.4 us
  other arithmetic: 43.5 us -> 0 us
  blocking collectives: 24.2 us -> 0 us
  starting transfers between devices: 16.2 us -> 0 us
  matrix products: 14.9 us -> 0 us
  between operations: 13.8 us -> 0.01 us
    all_gather x2 -> x0, waiting for transfers between devices: 396 us -> none  [the longest x1 376 us: body(): lax.all_gather(out_weight, 'ctx', axis=0, tiled=True)]
    pallas_call x0 -> x1, Pallas kernels: none -> 92.4 us  [body(): pl.pallas_call(kernel, out_shape=jax.ShapeDtypeStruct((T, NL), bf), in_sp...]
    pad x12 -> x0, local copies, waits for them, and re-layouts: 85 us -> none  [block_pass(): scanned = lax.associative_scan(chain, (steps, ends), axis=2)[1]]
    slice x26 -> x0, local copies, waits for them, and re-layouts: 58.5 us -> none  [the longest x24 48 us: block_pass(): scanned = lax.associative_scan(chain, (steps, ends), axis=2)[1]]
    add x24 -> x0, other arithmetic: 27.8 us -> none  [the longest x14 16.1 us: chain(): return (earlier[0] * later[0], earlier[1] * later[0] + later[1])]
    all_to_all x1 -> x0, blocking collectives: 24.2 us -> none  [body(): lax.all_to_all(convolved_ch, 'ctx', split_axis=1, concat_axis=0, tiled=True)]
    dot_general x4 -> x0, matrix products: 14.9 us -> none  [the longest x1 9.24 us: body(): jnp.dot(gathered, lax.all_gather(out_weight, 'ctx', axis=0, tiled=True),...]
    all_to_all x1 -> x0, starting transfers between devices: 12.5 us -> none  [body(): lax.all_to_all(product.T, 'ctx', split_axis=0, concat_axis=1, tiled=True)]
  transfers between devices with their start and end apart: 4 -> 0, of which waited for: 3 -> 0; matrix products, arithmetic and copies ran while one was open for 2% -> 0% of each run, Pallas kernels for 0% -> 0%
where the time goes in v1:
time: 94.5 us; the launch traced here: 94.3 us
  Pallas kernels  92.4 us (98%)
  local copies, waits for them, and re-layouts  1.88 us (2%)
    pallas_call x1, Pallas kernels, body(): pl.pallas_call(kernel, out_shape=jax.ShapeDtypeStruct((T, NL), bf), in_sp...  92.4 us

profile of v1, /device:TPU:8, one launch (start us, length us, event | category | flops | bytes accessed | tf_op | source)
XLA Modules:
  0.0 94.3 jit_solution(15615542661536030900)
XLA Ops:
  0.0 92.4 %mixer.1 = bf16[128,2048]{1,0:T(8,128)(2,1)} custom-call(s32[1,128]{1,0:T(1,128)} %bitcast.5, f32[3,3,1024]{2,1,0:T(4,128)} %taps_ref.1, f32[16,1024]{1,0:T(8,128)} %rates_ref.1, f32[16,1024]{1,0:T(8,128)} %res_ref.1, f32[1,1024]{1,0:T(1,128)} %bitcast.4, bf16[3,512,1024]{2,1,0:T(8,128)(2,1)} %bitcast.3, bf16[64,2048]{1,0:T(8,128)(2,1)} %w_hbm.1), custom_call_target="tpu_custom_call" | custom-call | tf_op jit(solution)/shard_map/mixer/pallas_call | solution.py:474
  92.4 1.9 %copy.9 = bf16[128,2048]{1,0:T(8,128)(2,1)} copy(bf16[128,2048]{1,0:T(8,128)(2,1)} %mixer.1) | data formatting | bytes 1048576

commit v2 on v1

--- a/solution.py
+++ b/solution.py
@@ -15,12 +15,26 @@
 R = 16
 KS = 64
 NL = 2048
+NW = 4
+WW = NL // NW
+PAIRED = (0, 1)
+W_ORDER = (2, 3, 0, 1)
+W_STOPS = (
+    ((2, 0), (3, 0)),
+    ((2, 1), (3, 1), (0, 0), (1, 0)),
+    ((2, 2), (3, 2), (0, 1)),
+    ((1, 1), (2, 3), (3, 3), (0, 2)),
+    ((1, 2), (2, 4), (3, 4), (0, 3)),
+    ((1, 3), (0, 4)),
+    ((1, 4),),
+)
 NCHUNK = 8
 CW = NL // NCHUNK
 HW = CW // 2
-PAIRED = (0, 1, 2, 3)
-SHARD = (4, 5, 6, 7)
-ORDER = (0, 4, 1, 5, 2, 6, 3, 7)
+PER = NCHUNK // NW
+LAG2, LAG3 = 3, 6
+ORDER = tuple(n * PER + k for n in W_ORDER for k in range(PER))
+FAR_FIRST = tuple(sorted(range(1, PLANE), key=lambda d: abs(d - PLANE // 2)))
 
 
 def right_steps(n):
@@ -32,11 +46,11 @@
 
 
 def kernel(
-    ids_ref, taps_ref, rates_ref, res_ref, skip_ref, table_hbm, w_hbm, out_ref,
-    table, rows, halo_out, halo_in, q_ref, u_ref, u2d, z2d, rate_t, coef_t,
+    ids_hbm, taps_hbm, rates_hbm, res_hbm, skip_hbm, table_hbm, w_hbm, out_hbm,
+    out_ref,     ids_ref, taps_ref, rates_ref, res_ref, skip_ref, table, rows, halo_out, halo_in, q_ref, u_ref, u2d, z2d, rate_t, coef_t,
     e_out, e_in, s_out, s_in, tot_out, tot_in, ybf, ybuf, wbuf,
     o_stage, relay_in, f32_part, fin_out, fin_in,
-    sem_table, sem_w, halo_s, halo_r, e_s, e_r, t_s, t_r, b_s, b_r,
+    sem_out, sem_in, sem_table, sem_w, halo_s, halo_r, e_s, e_r, t_s, t_r, b_s, b_r,
     yx_s, yx_r, yc_s, yc_r, yl_s, wx_s, wx_r, wz_s, wz_r,
     rl_s, rl_r, fn_s, fn_r,
 ):
@@ -61,7 +75,7 @@
 
     bar = pltpu.get_barrier_semaphore()
     n_peers = 0
-    for d in range(1, PLANE):
+    for d in FAR_FIRST:
         pl.semaphore_signal(bar, inc=1, device_id=in_plane(lax.rem(p + d, PLANE)), device_id_type=MESH)
         n_peers += 1
     for dy in range(NY):
@@ -83,13 +97,23 @@
 
     def w_copy(n):
         return pltpu.make_async_copy(
-            w_hbm.at[:, pl.ds(n * CW, CW)], wbuf.at[n, pl.ds(own_row, KS), :], sem_w.at[n]
+            w_hbm.at[:, pl.ds(n * WW, WW)], wbuf.at[n, pl.ds(own_row, KS), :], sem_w.at[n]
         )
 
+    small = [
+        pltpu.make_async_copy(src, dst, sem_in.at[k])
+        for k, (src, dst) in enumerate((
+            (ids_hbm, ids_ref), (rates_hbm, rates_ref), (res_hbm, res_ref), (taps_hbm, taps_ref), (skip_hbm, skip_ref)
+        ))
+    ]
+    for copy in small:
+        copy.start()
     for w in (1, 2, 0):
         table_copy(w).start()
-    for n in ORDER:
+    for n in W_ORDER:
         w_copy(n).start()
+    for copy in small:
+        copy.wait()
 
     for lt in range(LT):
         cols = slice(lt * 128, (lt + 1) * 128)
@@ -139,7 +163,7 @@
         ref = w_rows(n, zat(-s if direction == 0 else s))
         return rdma(ref, ref, wz_s.at[n, direction, s], wz_r.at[n, direction, s], zr if direction == 0 else zl)
 
-    for n in ORDER:
+    for n in W_ORDER:
         w_copy(n).wait()
         if n in PAIRED:
             x_copy(n, 0).start()
@@ -167,10 +191,8 @@
             for d in range(NZ):
                 x_copy(n, d).wait_recv()
 
-    ops = sorted(
-        [(2 * (n % 4) + s, n % 4, n, s) for n in ORDER for s in range(5)]
-    )
-    ops = [(n, s) for _, _, n, s in ops]
+    ops = [op for stop in W_STOPS for op in stop]
+    counts = [sum(len(stop) for stop in W_STOPS[:k + 1]) for k in range(len(W_STOPS))]
     state = {"next": 0}
 
     def advance(upto):
@@ -178,8 +200,10 @@
             w_op(*ops[state["next"]])
             state["next"] += 1
 
-    def advance_to(k):
-        advance(lambda idx, op: idx < k)
+    def advance_to(stop):
+        advance(lambda idx, op: idx < counts[stop])
+
+    advance_to(0)
 
     def features(t0, n):
         for lt in range(LT):
@@ -232,10 +256,10 @@
         frm = lax.rem(p + d, PLANE)
         return rdma(e_out.at[frm], e_in.at[frm], e_s.at[d], e_r.at[frm], in_plane(frm))
 
-    for d in range(1, PLANE):
+    for d in FAR_FIRST:
         e_copy(d).start()
     e_in[p] = e_out[p]
-    advance_to(4)
+    advance_to(1)
     for d in range(1, PLANE):
         e_from(d).wait_recv()
 
@@ -259,7 +283,7 @@
     for d in range(1, NY):
         t_copy(d).start()
     tot_in[y] = pref
-    advance_to(8)
+    advance_to(2)
     for d in range(1, NY):
         t_from(d).wait_recv()
     carry = zero
@@ -277,10 +301,10 @@
         frm = lax.rem(p + d, PLANE)
         return rdma(s_out.at[frm], s_in.at[frm], b_s.at[d], b_r.at[frm], in_plane(frm))
 
-    for d in range(1, PLANE):
+    for d in FAR_FIRST:
         s_copy(d).start()
     s_in[p] = s_out[p]
-    advance_to(12)
+    advance_to(3)
     for d in range(1, PLANE):
         s_from(d).wait_recv()
 
@@ -330,7 +354,13 @@
         y_own().start()
         y_own().wait()
 
-    advance_to(16)
+    halo.wait_send()
+    for d in range(1, PLANE):
+        e_copy(d).wait_send()
+        s_copy(d).wait_send()
+    for d in range(1, NY):
+        t_copy(d).wait_send()
+    advance_to(4)
     sib = at(y, c + 1 - 2 * core)
 
     def y_cross(k):
@@ -349,6 +379,7 @@
             rdma(ybf, ybuf.at[slot], yx_s.at[k], yx_r.at[slot], at(slot, y)).wait_recv()
 
         y_cross(k).start()
+    advance_to(5)
     for k in range(2):
         y_cross_from(k).wait_recv()
 
@@ -361,13 +392,21 @@
     def final(n, side):
         return rdma(fin_out.at[n, side], fin_in.at[n, side], fn_s.at[n, side], fn_r.at[n, side], (yr, yl)[side])
 
+    def out_copy(n):
+        cols = pl.ds(n * CW, CW)
+        return pltpu.make_async_copy(out_ref.at[:, cols], out_hbm.at[:, cols], sem_out.at[n])
+
     def product(n, d):
         block = ybuf[lax.rem(y + d, NY)]
-        return jnp.dot(block, wbuf[n], preferred_element_type=f32)
+        return jnp.dot(
+            block, wbuf[n // PER, :, (n % PER) * CW:(n % PER + 1) * CW], preferred_element_type=f32
+        )
 
     def stage1(n):
-        advance(lambda idx, op: any(m == n for m, _ in ops[idx:]))
-        w_done(n)
+        wn, half = n // PER, n % PER
+        if half == 0:
+            advance(lambda idx, op: any(m == wn for m, _ in ops[idx:]))
+            w_done(wn)
         far = product(n, 2)
         o_stage[n, 0] = far[:, A].astype(jnp.bfloat16)
         o_stage[n, 1] = far[:, B].astype(jnp.bfloat16)
@@ -392,23 +431,26 @@
         final(n, 1).wait_recv()
         total = f32_part[n, 2] + fin_in[n, 0].astype(f32) + fin_in[n, 1].astype(f32)
         out_ref[:, n * CW:(n + 1) * CW] = total.astype(jnp.bfloat16)
-
-    for k, n in enumerate(ORDER):
-        stage1(n)
-        if k >= 1:
-            stage2(ORDER[k - 1])
-        if k >= 3:
-            stage3(ORDER[k - 3])
-    stage2(ORDER[-1])
-    for n in ORDER[-3:]:
-        stage3(n)
-
-    halo.wait_send()
-    for d in range(1, PLANE):
-        e_copy(d).wait_send()
-        s_copy(d).wait_send()
-    for d in range(1, NY):
-        t_copy(d).wait_send()
+        out_copy(n).start()
+
+    def w_sent(n):
+        for direction, steps in ((0, right_steps(n)), (1, left_steps(n))):
+            for s in range(steps):
+                ring(n, direction, s).wait_send()
+        for d in range(1 if n in PAIRED else NZ):
+            x_copy(n, d).wait_send()
+
+    for k in range(NCHUNK + LAG3):
+        if k < NCHUNK:
+            stage1(ORDER[k])
+        if 0 <= k - LAG2 < NCHUNK:
+            stage2(ORDER[k - LAG2])
+        if k == NCHUNK:
+            for n in W_ORDER:
+                w_sent(n)
+        if k >= LAG3:
+            stage3(ORDER[k - LAG3])
+
     for h in range(2):
         @pl.when(jnp.logical_not(is_self(h)))
         def _():
@@ -416,26 +458,24 @@
     for k in range(2):
         y_cross(k).wait_send()
     for n in ORDER:
-        for direction, steps in ((0, right_steps(n)), (1, left_steps(n))):
-            for s in range(steps):
-                ring(n, direction, s).wait_send()
-        if n in PAIRED:
-            x_copy(n, 0).wait_send()
-        else:
-            for d in range(NZ):
-                x_copy(n, d).wait_send()
         for side in range(2):
             relay(n, side).wait_send()
             final(n, side).wait_send()
+        out_copy(n).wait()
 
 
 def body(base_ids, base_table, short_taps, mode_rates, mode_residues, skip_gain, out_weight):
     f32, bf = jnp.float32, jnp.bfloat16
     table = jnp.transpose(base_table, (1, 0, 2))
-    vmem = pl.BlockSpec(memory_space=pltpu.VMEM)
-    hbm = pl.BlockSpec(memory_space=pl.ANY)
+    hbm = pl.BlockSpec(memory_space=pltpu.HBM)
     dma = pltpu.SemaphoreType.DMA
     scratch = [
+        pltpu.VMEM((T, NL), bf),
+        pltpu.VMEM((1, T), jnp.int32),
+        pltpu.VMEM((3, 3, CL), f32),
+        pltpu.VMEM((R, CL), f32),
+        pltpu.VMEM((R, CL), f32),
+        pltpu.VMEM((1, CL), f32),
         pltpu.VMEM((3, 512, CL), bf),
         pltpu.VMEM((3, T + 8, CL), f32),
         pltpu.VMEM((3, 2, CL), f32),
@@ -454,28 +494,28 @@
         pltpu.VMEM((NY, LT, 128), f32),
         pltpu.VMEM((T, CL), bf),
         pltpu.VMEM((NY, T, CL), bf),
-        pltpu.VMEM((NCHUNK, CL, CW), bf),
+        pltpu.VMEM((NW, CL, WW), bf),
         pltpu.VMEM((NCHUNK, 2, T, HW), bf),
         pltpu.VMEM((NCHUNK, 2, T, HW), bf),
         pltpu.VMEM((NCHUNK, 3, T, CW), f32),
         pltpu.VMEM((NCHUNK, 2, T, CW), bf),
         pltpu.VMEM((NCHUNK, 2, T, CW), bf),
-        dma((3,)), dma((NCHUNK,)),
+        dma((NCHUNK,)), dma((5,)), dma((3,)), dma((NW,)),
         dma, dma,
         dma((PLANE,)), dma((PLANE,)),
         dma((NY,)), dma((NY,)),
         dma((PLANE,)), dma((PLANE,)),
         dma((2,)), dma((NY,)), dma((2,)), dma((NY,)), dma,
-        dma((NCHUNK, NZ)), dma((NCHUNK, NZ)),
-        dma((NCHUNK, 2, 4)), dma((NCHUNK, 2, 4)),
+        dma((NW, NZ)), dma((NW, NZ)),
+        dma((NW, 2, 4)), dma((NW, 2, 4)),
         dma((NCHUNK, 2)), dma((NCHUNK, 2)),
         dma((NCHUNK, 2)), dma((NCHUNK, 2)),
     ]
     return pl.pallas_call(
         kernel,
         out_shape=jax.ShapeDtypeStruct((T, NL), bf),
-        in_specs=[vmem] * 5 + [hbm] * 2,
-        out_specs=vmem,
+        in_specs=[hbm] * 7,
+        out_specs=hbm,
         scratch_shapes=scratch,
         compiler_params=pltpu.CompilerParams(
             collective_id=0, has_side_effects=True, vmem_limit_bytes=56 * 2**20

time: 94.5 us -> 72.3 us (0.77)
  the two profiles are of different devices: /device:TPU:8 before, /device:TPU:1 now
where the time goes in v2:
time: 72.3 us; the launch traced here: 72.2 us
  Pallas kernels  70.3 us (97%)
  local copies, waits for them, and re-layouts  1.88 us (3%)
    pallas_call x1, Pallas kernels, body(): pl.pallas_call(kernel, out_shape=jax.ShapeDtypeStruct((T, NL), bf), in_sp...  70.3 us
    unnamed x1, local copies, waits for them, and re-layouts  1.88 us

profile of v2, /device:TPU:1, one launch (start us, length us, event | category | flops | bytes accessed | tf_op | source)
XLA Modules:
  0.0 72.2 jit_solution(8052582977112718144)
XLA Ops:
  0.0 70.3 %mixer.1 = bf16[128,2048]{1,0:T(8,128)(2,1)} custom-call(s32[1,128]{1,0:T(1,128)} %bitcast.5, f32[3,3,1024]{2,1,0:T(4,128)} %taps_hbm.1, f32[16,1024]{1,0:T(8,128)} %rates_hbm.1, f32[16,1024]{1,0:T(8,128)} %res_hbm.1, f32[1,1024]{1,0:T(1,128)} %bitcast.4, bf16[3,512,1024]{2,1,0:T(8,128)(2,1)} %bitcast.3, bf16[64,2048]{1,0:T(8,128)(2,1)} %w_hbm.1), custom_call_target="tpu_custom_call" | custom-call | tf_op jit(solution)/shard_map/mixer/pallas_call | solution.py:514
  70.3 1.9 %copy.9 = bf16[128,2048]{1,0:T(8,128)(2,1)} copy(bf16[128,2048]{1,0:T(8,128)(2,1)} %mixer.1) | data formatting | bytes 1048576

commit v3 on v2

--- a/solution.py
+++ b/solution.py
@@ -18,14 +18,18 @@
 NW = 4
 WW = NL // NW
 PAIRED = (0, 1)
-W_ORDER = (2, 3, 0, 1)
+W_ORDER = (0, 2, 3, 1)
 W_STOPS = (
-    ((2, 0), (3, 0)),
-    ((2, 1), (3, 1), (0, 0), (1, 0)),
-    ((2, 2), (3, 2), (0, 1)),
-    ((1, 1), (2, 3), (3, 3), (0, 2)),
-    ((1, 2), (2, 4), (3, 4), (0, 3)),
-    ((1, 3), (0, 4)),
+    ((2, 0), (3, 0),),
+    ((0, 0), (2, 1), (3, 1),),
+    ((0, 1),),
+    ((2, 2), (3, 2), (0, 2), (1, 0),),
+    ((2, 3), (3, 3), (0, 3), (1, 1),),
+    ((0, 4), (2, 4), (3, 4), (1, 2),),
+)
+W_ROUNDS = (
+    ((1, 3),),
+    (),
     ((1, 4),),
 )
 NCHUNK = 8
@@ -33,7 +37,6 @@
 HW = CW // 2
 PER = NCHUNK // NW
 LAG2, LAG3 = 3, 6
-ORDER = tuple(n * PER + k for n in W_ORDER for k in range(PER))
 FAR_FIRST = tuple(sorted(range(1, PLANE), key=lambda d: abs(d - PLANE // 2)))
 
 
@@ -50,7 +53,7 @@
     out_ref,     ids_ref, taps_ref, rates_ref, res_ref, skip_ref, table, rows, halo_out, halo_in, q_ref, u_ref, u2d, z2d, rate_t, coef_t,
     e_out, e_in, s_out, s_in, tot_out, tot_in, ybf, ybuf, wbuf,
     o_stage, relay_in, f32_part, fin_out, fin_in,
-    sem_out, sem_in, sem_table, sem_w, halo_s, halo_r, e_s, e_r, t_s, t_r, b_s, b_r,
+    far_sem, sem_out, sem_in, sem_table, sem_w, halo_s, halo_r, e_s, e_r, t_s, t_r, b_s, b_r,
     yx_s, yx_r, yc_s, yc_r, yl_s, wx_s, wx_r, wz_s, wz_r,
     rl_s, rl_r, fn_s, fn_r,
 ):
@@ -73,22 +76,23 @@
             src_ref=src, dst_ref=dst, send_sem=ss, recv_sem=rs, device_id=dev, device_id_type=MESH
         )
 
+    def zdev(d):
+        return in_plane(lax.rem(z + d + NZ, NZ) * NX + xl)
+
+    nxt, prv = lax.rem(i + 1, NY * PLANE), lax.rem(i + NY * PLANE - 1, NY * PLANE)
+    partner = in_plane(p + 1 - 2 * xl)
+    block = [
+        at(lax.rem(y + 1, NY), c), at(lax.rem(y + NY - 1, NY), c),
+        at(y, c + 1 - 2 * lax.rem(c, 2)), at(y, lax.rem(c + 2, NCH)),
+    ]
+
+    def greet(sem, devices):
+        for dev in devices:
+            pl.semaphore_signal(sem, inc=1, device_id=dev, device_id_type=MESH)
+
     bar = pltpu.get_barrier_semaphore()
-    n_peers = 0
-    for d in FAR_FIRST:
-        pl.semaphore_signal(bar, inc=1, device_id=in_plane(lax.rem(p + d, PLANE)), device_id_type=MESH)
-        n_peers += 1
-    for dy in range(NY):
-        for dc in range(NCH):
-            if dy or dc:
-                pl.semaphore_signal(
-                    bar, inc=1, device_id=at(lax.rem(y + dy, NY), lax.rem(c + dc, NCH)), device_id_type=MESH
-                )
-                n_peers += 1
-    nxt, prv = lax.rem(i + 1, NY * PLANE), lax.rem(i + NY * PLANE - 1, NY * PLANE)
-    for other in (nxt, prv):
-        pl.semaphore_signal(bar, inc=1, device_id=(other, c), device_id_type=MESH)
-        n_peers += 1
+    near = [zdev(1), zdev(-1), partner, (nxt, c), (prv, c)] + block
+    greet(bar, near)
 
     def table_copy(w):
         return pltpu.make_async_copy(table_hbm.at[w], table.at[w], sem_table.at[w])
@@ -134,12 +138,13 @@
             rows[w, 8:, cols] = jnp.dot(onehot, table[w, :, cols], preferred_element_type=f32)
         halo_out[w, :, :] = rows[w, 8 + T - 2:, :]
 
-    pl.semaphore_wait(bar, n_peers)
+    pl.semaphore_wait(bar, len(near))
+    greet(far_sem.at[0], [zdev(1), zdev(-1)])
+    greet(far_sem.at[3], block)
 
     halo = rdma(halo_out, halo_in, halo_s, halo_r, (nxt, c))
     halo.start()
 
-    partner = in_plane(p + 1 - 2 * xl)
     zr = in_plane(lax.rem(z + 1, NZ) * NX + xl)
     zl = in_plane(lax.rem(z + NZ - 1, NZ) * NX + xl)
 
@@ -163,7 +168,7 @@
         ref = w_rows(n, zat(-s if direction == 0 else s))
         return rdma(ref, ref, wz_s.at[n, direction, s], wz_r.at[n, direction, s], zr if direction == 0 else zl)
 
-    for n in W_ORDER:
+    for n in range(NW):
         w_copy(n).wait()
         if n in PAIRED:
             x_copy(n, 0).start()
@@ -191,19 +196,13 @@
             for d in range(NZ):
                 x_copy(n, d).wait_recv()
 
-    ops = [op for stop in W_STOPS for op in stop]
-    counts = [sum(len(stop) for stop in W_STOPS[:k + 1]) for k in range(len(W_STOPS))]
-    state = {"next": 0}
-
-    def advance(upto):
-        while state["next"] < len(ops) and upto(state["next"], ops[state["next"]]):
-            w_op(*ops[state["next"]])
-            state["next"] += 1
-
     def advance_to(stop):
-        advance(lambda idx, op: idx < counts[stop])
+        for op in W_STOPS[stop]:
+            w_op(*op)
 
     advance_to(0)
+    pl.semaphore_wait(far_sem.at[0], 2)
+    greet(far_sem.at[1], [zdev(2), zdev(-2)])
 
     def features(t0, n):
         for lt in range(LT):
@@ -238,6 +237,10 @@
     tail = scan_states(1, T // 8, (zero,) * R)
     for r in range(R):
         e_out[r] = tail[r]
+    pl.semaphore_wait(far_sem.at[1], 2)
+    greet(far_sem.at[2], [partner])
+    pl.semaphore_wait(far_sem.at[3], 4)
+    greet(far_sem.at[4], block)
 
     halo.wait_recv()
     keep = jnp.where(i == 0, 0.0, 1.0).astype(f32)
@@ -248,6 +251,8 @@
     for r in range(R):
         e_out[r] = e_out[r] + jnp.exp(-float(T - 8) * rate[r]) * head[r]
 
+    pl.semaphore_wait(far_sem.at[2], 1)
+
     def e_copy(d):
         to = lax.rem(p + d, PLANE)
         return rdma(e_out.at[to], e_in.at[p], e_s.at[d], e_r.at[p], in_plane(to))
@@ -262,6 +267,9 @@
     advance_to(1)
     for d in range(1, PLANE):
         e_from(d).wait_recv()
+
+    pl.semaphore_wait(far_sem.at[4], 4)
+    greet(far_sem.at[5], block)
 
     my_rate = rate_t[pl.ds(pl.multiple_of(p * LT, LT), LT), :]
     dev_decay = jnp.exp(-float(T) * my_rate)
@@ -330,14 +338,19 @@
         gated = q_ref[:, cols] * (conv + skip_ref[:, cols] * u_ref[:, cols])
         ybf[:, cols] = gated.astype(jnp.bfloat16)
 
+    pl.semaphore_wait(far_sem.at[5], 4)
+
     odd = lax.rem(y, 2)
     core = lax.rem(c, 2)
 
+    def y_rows(slot):
+        return pl.ds(pl.multiple_of(slot * T, T), T)
+
     def y_copy(h):
-        return rdma(ybf, ybuf.at[y], yx_s.at[h], yx_r.at[y], at(c, 2 * h + odd))
+        return rdma(ybf, ybuf.at[y_rows(y)], yx_s.at[h], yx_r.at[y], at(c, 2 * h + odd))
 
     def y_own():
-        return pltpu.make_async_copy(ybf, ybuf.at[y], yl_s)
+        return pltpu.make_async_copy(ybf, ybuf.at[y_rows(y)], yl_s)
 
     def is_self(h):
         return jnp.logical_and(y == c, c // 2 == h)
@@ -365,18 +378,18 @@
 
     def y_cross(k):
         slot = 2 * k + core
-        return rdma(ybuf.at[slot], ybuf.at[slot], yc_s.at[k], yc_r.at[slot], sib)
+        return rdma(ybuf.at[y_rows(slot)], ybuf.at[y_rows(slot)], yc_s.at[k], yc_r.at[slot], sib)
 
     def y_cross_from(k):
         slot = 2 * k + 1 - core
-        return rdma(ybuf.at[slot], ybuf.at[slot], yc_s.at[k], yc_r.at[slot], sib)
+        return rdma(ybuf.at[y_rows(slot)], ybuf.at[y_rows(slot)], yc_s.at[k], yc_r.at[slot], sib)
 
     for k in range(2):
         slot = 2 * k + core
 
         @pl.when(jnp.logical_not(jnp.logical_and(slot == y, c == y)))
         def _():
-            rdma(ybf, ybuf.at[slot], yx_s.at[k], yx_r.at[slot], at(slot, y)).wait_recv()
+            rdma(ybf, ybuf.at[y_rows(slot)], yx_s.at[k], yx_r.at[slot], at(slot, y)).wait_recv()
 
         y_cross(k).start()
     advance_to(5)
@@ -392,45 +405,46 @@
     def final(n, side):
         return rdma(fin_out.at[n, side], fin_in.at[n, side], fn_s.at[n, side], fn_r.at[n, side], (yr, yl)[side])
 
+    def out_cols(n):
+        return pl.ds(pl.multiple_of(n * CW, CW), CW)
+
     def out_copy(n):
-        cols = pl.ds(n * CW, CW)
-        return pltpu.make_async_copy(out_ref.at[:, cols], out_hbm.at[:, cols], sem_out.at[n])
-
-    def product(n, d):
-        block = ybuf[lax.rem(y + d, NY)]
-        return jnp.dot(
-            block, wbuf[n // PER, :, (n % PER) * CW:(n % PER + 1) * CW], preferred_element_type=f32
-        )
-
-    def stage1(n):
-        wn, half = n // PER, n % PER
-        if half == 0:
-            advance(lambda idx, op: any(m == wn for m, _ in ops[idx:]))
-            w_done(wn)
-        far = product(n, 2)
-        o_stage[n, 0] = far[:, A].astype(jnp.bfloat16)
-        o_stage[n, 1] = far[:, B].astype(jnp.bfloat16)
+        return pltpu.make_async_copy(out_ref.at[:, out_cols(n)], out_hbm.at[:, out_cols(n)], sem_out.at[n])
+
+    right, far, left = lax.rem(y + 1, NY), lax.rem(y + 2, NY), lax.rem(y + 3, NY)
+
+    def chunk(k):
+        wn = sum(jnp.where(k // PER == j, m, 0) for j, m in enumerate(W_ORDER))
+        return wn, wn * PER + lax.rem(k, PER)
+
+    def stage1(k):
+        wn, n = chunk(k)
+        cols = pl.ds(pl.multiple_of(lax.rem(k, PER) * CW, CW), CW)
+        prod = jnp.dot(ybuf[...], wbuf[wn, :, cols], preferred_element_type=f32)
+        f32_part[n] = prod.reshape(NY, T, CW)
+        opposite = f32_part[n, far].astype(jnp.bfloat16)
+        o_stage[n, 0] = opposite[:, A]
+        o_stage[n, 1] = opposite[:, B]
         relay(n, 0).start()
         relay(n, 1).start()
-        f32_part[n, 0] = product(n, 1)
-        f32_part[n, 1] = product(n, 3)
-        f32_part[n, 2] = product(n, 0)
-
-    def stage2(n):
+
+    def stage2(k):
+        _, n = chunk(k)
         relay(n, 0).wait_recv()
-        fin_out[n, 0, :, A] = (f32_part[n, 0, :, A] + relay_in[n, 0].astype(f32)).astype(jnp.bfloat16)
-        fin_out[n, 0, :, B] = f32_part[n, 0, :, B].astype(jnp.bfloat16)
+        fin_out[n, 0, :, A] = (f32_part[n, right, :, A] + relay_in[n, 0].astype(f32)).astype(jnp.bfloat16)
+        fin_out[n, 0, :, B] = f32_part[n, right, :, B].astype(jnp.bfloat16)
         final(n, 0).start()
         relay(n, 1).wait_recv()
-        fin_out[n, 1, :, A] = f32_part[n, 1, :, A].astype(jnp.bfloat16)
-        fin_out[n, 1, :, B] = (f32_part[n, 1, :, B] + relay_in[n, 1].astype(f32)).astype(jnp.bfloat16)
+        fin_out[n, 1, :, A] = f32_part[n, left, :, A].astype(jnp.bfloat16)
+        fin_out[n, 1, :, B] = (f32_part[n, left, :, B] + relay_in[n, 1].astype(f32)).astype(jnp.bfloat16)
         final(n, 1).start()
 
-    def stage3(n):
+    def stage3(k):
+        _, n = chunk(k)
         final(n, 0).wait_recv()
         final(n, 1).wait_recv()
-        total = f32_part[n, 2] + fin_in[n, 0].astype(f32) + fin_in[n, 1].astype(f32)
-        out_ref[:, n * CW:(n + 1) * CW] = total.astype(jnp.bfloat16)
+        total = f32_part[n, y] + fin_in[n, 0].astype(f32) + fin_in[n, 1].astype(f32)
+        out_ref[:, out_cols(n)] = total.astype(jnp.bfloat16)
         out_copy(n).start()
 
     def w_sent(n):
@@ -440,16 +454,36 @@
         for d in range(1 if n in PAIRED else NZ):
             x_copy(n, d).wait_send()
 
-    for k in range(NCHUNK + LAG3):
-        if k < NCHUNK:
-            stage1(ORDER[k])
-        if 0 <= k - LAG2 < NCHUNK:
-            stage2(ORDER[k - LAG2])
-        if k == NCHUNK:
-            for n in W_ORDER:
-                w_sent(n)
-        if k >= LAG3:
-            stage3(ORDER[k - LAG3])
+    def round_(k, carry):
+        for j, wn in enumerate(W_ORDER):
+            @pl.when(k == j * PER)
+            def _():
+                w_done(wn)
+
+        @pl.when(k < NCHUNK)
+        def _():
+            stage1(k)
+
+        for r, stop in enumerate(W_ROUNDS):
+            if stop:
+                @pl.when(k == r)
+                def _():
+                    for op in stop:
+                        w_op(*op)
+
+        @pl.when(jnp.logical_and(k >= LAG2, k < NCHUNK + LAG2))
+        def _():
+            stage2(k - LAG2)
+
+        @pl.when(k >= LAG3)
+        def _():
+            stage3(k - LAG3)
+
+        return carry
+
+    lax.fori_loop(0, NCHUNK + LAG3, round_, 0)
+    for n in W_ORDER:
+        w_sent(n)
 
     for h in range(2):
         @pl.when(jnp.logical_not(is_self(h)))
@@ -457,7 +491,7 @@
             y_copy(h).wait_send()
     for k in range(2):
         y_cross(k).wait_send()
-    for n in ORDER:
+    for n in range(NCHUNK):
         for side in range(2):
             relay(n, side).wait_send()
             final(n, side).wait_send()
@@ -493,13 +527,14 @@
         pltpu.VMEM((LT, 128), f32),
         pltpu.VMEM((NY, LT, 128), f32),
         pltpu.VMEM((T, CL), bf),
-        pltpu.VMEM((NY, T, CL), bf),
+        pltpu.VMEM((NY * T, CL), bf),
         pltpu.VMEM((NW, CL, WW), bf),
         pltpu.VMEM((NCHUNK, 2, T, HW), bf),
         pltpu.VMEM((NCHUNK, 2, T, HW), bf),
-        pltpu.VMEM((NCHUNK, 3, T, CW), f32),
+        pltpu.VMEM((NCHUNK, NY, T, CW), f32),
         pltpu.VMEM((NCHUNK, 2, T, CW), bf),
         pltpu.VMEM((NCHUNK, 2, T, CW), bf),
+        pltpu.SemaphoreType.REGULAR((6,)),
         dma((NCHUNK,)), dma((5,)), dma((3,)), dma((NW,)),
         dma, dma,
         dma((PLANE,)), dma((PLANE,)),

time: 72.3 us -> 69.7 us (0.964)
  the two profiles are of different devices: /device:TPU:1 before, /device:TPU:8 now
where the time goes in v3:
time: 69.7 us; the launch traced here: 69.3 us
  Pallas kernels  67.4 us (97%)
  local copies, waits for them, and re-layouts  1.88 us (3%)
    pallas_call x1, Pallas kernels, body(): pl.pallas_call(kernel, out_shape=jax.ShapeDtypeStruct((T, NL), bf), in_sp...  67.4 us
    unnamed x1, local copies, waits for them, and re-layouts  1.88 us

profile of v3, /device:TPU:8, one launch (start us, length us, event | category | flops | bytes accessed | tf_op | source)
XLA Modules:
  0.0 69.3 jit_solution(875858572472632079)
XLA Ops:
  0.0 67.4 %mixer.1 = bf16[128,2048]{1,0:T(8,128)(2,1)} custom-call(s32[1,128]{1,0:T(1,128)} %bitcast.5, f32[3,3,1024]{2,1,0:T(4,128)} %taps_hbm.1, f32[16,1024]{1,0:T(8,128)} %rates_hbm.1, f32[16,1024]{1,0:T(8,128)} %res_hbm.1, f32[1,1024]{1,0:T(1,128)} %bitcast.4, bf16[3,512,1024]{2,1,0:T(8,128)(2,1)} %bitcast.3, bf16[64,2048]{1,0:T(8,128)(2,1)} %w_hbm.1), custom_call_target="tpu_custom_call" | custom-call | tf_op jit(solution)/shard_map/mixer/pallas_call | solution.py:549
  67.4 1.9 %copy.9 = bf16[128,2048]{1,0:T(8,128)(2,1)} copy(bf16[128,2048]{1,0:T(8,128)(2,1)} %mixer.1) | data formatting | bytes 1048576

commit v4 on v3

--- a/solution.py
+++ b/solution.py
@@ -30,7 +30,10 @@
 W_ROUNDS = (
     ((1, 3),),
     (),
+    (),
     ((1, 4),),
+    (),
+    (),
 )
 NCHUNK = 8
 CW = NL // NCHUNK

time: 69.7 us -> 69 us (0.990)
  Pallas kernels: 67.4 us -> 66.3 us
    pallas_call x1, Pallas kernels: 67.4 us -> 66.3 us  [body(): pl.pallas_call(kernel, out_shape=jax.ShapeDtypeStruct((T, NL), bf), in_sp...]
where the time goes in v4:
time: 69 us; the launch traced here: 68.2 us
  Pallas kernels  66.3 us (96%)
  local copies, waits for them, and re-layouts  1.88 us (3%)
    pallas_call x1, Pallas kernels, body(): pl.pallas_call(kernel, out_shape=jax.ShapeDtypeStruct((T, NL), bf), in_sp...  66.3 us
    unnamed x1, local copies, waits for them, and re-layouts  1.88 us

profile of v4, /device:TPU:8, one launch (start us, length us, event | category | flops | bytes accessed | tf_op | source)
XLA Modules:
  0.0 68.2 jit_solution(13288138069868885360)
XLA Ops:
  0.0 66.3 %mixer.1 = bf16[128,2048]{1,0:T(8,128)(2,1)} custom-call(s32[1,128]{1,0:T(1,128)} %bitcast.5, f32[3,3,1024]{2,1,0:T(4,128)} %taps_hbm.1, f32[16,1024]{1,0:T(8,128)} %rates_hbm.1, f32[16,1024]{1,0:T(8,128)} %res_hbm.1, f32[1,1024]{1,0:T(1,128)} %bitcast.4, bf16[3,512,1024]{2,1,0:T(8,128)(2,1)} %bitcast.3, bf16[64,2048]{1,0:T(8,128)(2,1)} %w_hbm.1), custom_call_target="tpu_custom_call" | custom-call | tf_op jit(solution)/shard_map/mixer/pallas_call | solution.py:552
  66.3 1.9 %copy.9 = bf16[128,2048]{1,0:T(8,128)(2,1)} copy(bf16[128,2048]{1,0:T(8,128)(2,1)} %mixer.1) | data formatting | bytes 1048576

commit v5 on v4

--- a/solution.py
+++ b/solution.py
@@ -258,18 +258,13 @@
 
     def e_copy(d):
         to = lax.rem(p + d, PLANE)
-        return rdma(e_out.at[to], e_in.at[p], e_s.at[d], e_r.at[p], in_plane(to))
-
-    def e_from(d):
-        frm = lax.rem(p + d, PLANE)
-        return rdma(e_out.at[frm], e_in.at[frm], e_s.at[d], e_r.at[frm], in_plane(frm))
+        return rdma(e_out.at[to], e_in.at[p], e_s.at[d], e_r, in_plane(to))
 
     for d in FAR_FIRST:
         e_copy(d).start()
     e_in[p] = e_out[p]
     advance_to(1)
-    for d in range(1, PLANE):
-        e_from(d).wait_recv()
+    rdma(e_out.at[pl.ds(0, R - 1)], e_in.at[pl.ds(0, R - 1)], e_s.at[0], e_r, partner).wait_recv()
 
     pl.semaphore_wait(far_sem.at[4], 4)
     greet(far_sem.at[5], block)
@@ -291,7 +286,7 @@
         frm = lax.rem(y + d, NY)
         return rdma(tot_out, tot_in.at[frm], t_s.at[d], t_r.at[frm], at(frm, c))
 
-    for d in range(1, NY):
+    for d in (2, 1, 3):
         t_copy(d).start()
     tot_in[y] = pref
     advance_to(2)
@@ -306,18 +301,13 @@
 
     def s_copy(d):
         to = lax.rem(p + d, PLANE)
-        return rdma(s_out.at[to], s_in.at[p], b_s.at[d], b_r.at[p], in_plane(to))
-
-    def s_from(d):
-        frm = lax.rem(p + d, PLANE)
-        return rdma(s_out.at[frm], s_in.at[frm], b_s.at[d], b_r.at[frm], in_plane(frm))
+        return rdma(s_out.at[to], s_in.at[p], b_s.at[d], b_r, in_plane(to))
 
     for d in FAR_FIRST:
         s_copy(d).start()
     s_in[p] = s_out[p]
     advance_to(3)
-    for d in range(1, PLANE):
-        s_from(d).wait_recv()
+    rdma(s_out.at[pl.ds(0, R - 1)], s_in.at[pl.ds(0, R - 1)], b_s.at[0], b_r, partner).wait_recv()
 
     coef = [coef_t[r * LT:(r + 1) * LT, :] for r in range(R)]
 
@@ -540,9 +530,9 @@
         pltpu.SemaphoreType.REGULAR((6,)),
         dma((NCHUNK,)), dma((5,)), dma((3,)), dma((NW,)),
         dma, dma,
-        dma((PLANE,)), dma((PLANE,)),
+        dma((PLANE,)), dma,
         dma((NY,)), dma((NY,)),
-        dma((PLANE,)), dma((PLANE,)),
+        dma((PLANE,)), dma,
         dma((2,)), dma((NY,)), dma((2,)), dma((NY,)), dma,
         dma((NW, NZ)), dma((NW, NZ)),
         dma((NW, 2, 4)), dma((NW, 2, 4)),

time: 69 us -> 68.7 us (level)
  no operation moved by 1% of the time
where the time goes in v5:
time: 68.7 us; the launch traced here: 67.9 us
  Pallas kernels  66 us (96%)
  local copies, waits for them, and re-layouts  1.88 us (3%)
    pallas_call x1, Pallas kernels, body(): pl.pallas_call(kernel, out_shape=jax.ShapeDtypeStruct((T, NL), bf), in_sp...  66 us
    unnamed x1, local copies, waits for them, and re-layouts  1.88 us

profile of v5, /device:TPU:8, one launch (start us, length us, event | category | flops | bytes accessed | tf_op | source)
XLA Modules:
  0.0 67.9 jit_solution(7245362250305050772)
XLA Ops:
  0.0 66.0 %mixer.1 = bf16[128,2048]{1,0:T(8,128)(2,1)} custom-call(s32[1,128]{1,0:T(1,128)} %bitcast.5, f32[3,3,1024]{2,1,0:T(4,128)} %taps_hbm.1, f32[16,1024]{1,0:T(8,128)} %rates_hbm.1, f32[16,1024]{1,0:T(8,128)} %res_hbm.1, f32[1,1024]{1,0:T(1,128)} %bitcast.4, bf16[3,512,1024]{2,1,0:T(8,128)(2,1)} %bitcast.3, bf16[64,2048]{1,0:T(8,128)(2,1)} %w_hbm.1), custom_call_target="tpu_custom_call" | custom-call | tf_op jit(solution)/shard_map/mixer/pallas_call | solution.py:542
  66.0 1.9 %copy.9 = bf16[128,2048]{1,0:T(8,128)(2,1)} copy(bf16[128,2048]{1,0:T(8,128)(2,1)} %mixer.1) | data formatting | bytes 1048576
